TPU v7x, 32 devices: a whole 2x2x4 slice. The times are simulated.
32 devices in a mesh: gy: 4 (over y, core), gx: 8 (over z, x).
Axes of the slice: x: 2, y: 2, z: 4, core: 2. Of those that a mesh axis runs over, the one named last changes fastest.
Arguments:
- first_frame: float32 [128, 256, 128], P('gy', 'gx'), may hold values from -6 to 6
- second_frame: float32 [128, 256, 128], P('gy', 'gx'), may hold values from -6 to 6
- source_column: int32 [4, 8, 4, 1], P('gy', 'gx'), may hold values from 0 to 7; in each aligned block of 4 rows (0 to 3, 4 to 7, ..., all dimensions but the last counted through in order) at most 2 rows name the same one
Outputs:
- flow_field: float32 [3, 128, 256, 128], P(None, 'gy', 'gx')
Inputs may be any that keep to these rules, and one draw needn't show every extreme that they name: `source_column`: among the 4 bricks of one device at most 2 take the same source column, and in every draw some device has 2 that do.
All inputs are finite; a program needn't handle non-finite values.
Results may differ from a plain program's by a relative error of at most 0.0001.
Values sent between devices are 32-bit elements; how exact they have to be, the bound alone decides.
A program may use at most 384 MiB of HBM per device.

v0:
```python
import functools

import jax
import jax.numpy as jnp
from jax import lax
from jax.experimental import pallas as pl
from jax.experimental.pallas import tpu as pltpu
from jax.sharding import PartitionSpec as P

BRICK = 32
LEVELS = 4
TIKHONOV = 0.05
CONTRAST = 0.5
RELAXATION = 0.8
FLOOR = 1.0
LANES = 128
PAD = 8
BUFFERS = (4, 6, 6, 3)
EXCHANGES = (4, 5, 5, 2)
MESH = pl.DeviceIdType.MESH


def dot(a, b):
    return jnp.dot(a, b, preferred_element_type=jnp.float32)


def two_terms(x, axis):
    high = x.astype(jnp.bfloat16).astype(jnp.float32)
    return jnp.concatenate([high, x - high], axis=axis).astype(jnp.bfloat16)


def solve_three(t, diagonal, f):
    aa = t[0] + diagonal
    ab, ac, bc = t[1], t[2], t[4]
    bb = t[3] + diagonal
    cc = t[5] + diagonal
    c_aa = bb * cc - bc * bc
    c_ab = ac * bc - ab * cc
    c_ac = ab * bc - ac * bb
    c_bb = aa * cc - ac * ac
    c_bc = ab * ac - aa * bc
    c_cc = aa * bb - ab * ab
    inverse = 1.0 / (aa * c_aa + ab * c_ab + ac * c_ac)
    return (
        (c_aa * f[0] + c_ab * f[1] + c_ac * f[2]) * inverse,
        (c_ab * f[0] + c_bb * f[1] + c_bc * f[2]) * inverse,
        (c_ac * f[0] + c_bc * f[1] + c_cc * f[2]) * inverse,
    )


def apply_three(t, u):
    return (
        t[0] * u[0] + t[1] * u[1] + t[2] * u[2],
        t[1] * u[0] + t[3] * u[1] + t[4] * u[2],
        t[2] * u[0] + t[4] * u[1] + t[5] * u[2],
    )


def kernel(n_gy, n_gx, height, across, *refs):
    first, second, columns, wide_columns, out = refs[:5]
    refs = refs[1:]
    gathered, avg, avg_stage, avg_halo = refs[4:8]
    tensors = refs[8:12]
    sources = refs[12:16]
    iterates = refs[16:20]
    stages = refs[20:24]
    halos = refs[24:28]
    residues = refs[28:31]
    gather_send, gather_recv, halo_send, halo_recv, avg_send, avg_recv, own_sem = refs[31:38]
    packed, table, turn_table, table_send, table_recv = refs[38:]
    my_y, my_x = lax.axis_index("gy"), lax.axis_index("gx")
    bases = [sum(EXCHANGES[:l]) * 4 for l in range(LEVELS)]
    hs = [height >> l for l in range(LEVELS)]
    ws = [across >> l for l in range(LEVELS)]
    wqs = [max(w, 8) for w in ws]

    for l in range(LEVELS):
        u, w, wq, h = iterates[l], ws[l], wqs[l], hs[l]
        for b in range(EXCHANGES[l]):
            zero_row = jnp.zeros((3, wq + 2 * PAD, LANES), jnp.float32)
            u[b, :, 0] = zero_row
            u[b, :, h + 1] = zero_row
            halos[l][b] = jnp.zeros(halos[l].shape[1:], jnp.float32)
    iterates[LEVELS - 1][...] = jnp.zeros(iterates[LEVELS - 1].shape, jnp.float32)
    avg[0] = jnp.zeros(avg.shape[1:], jnp.float32)
    avg[height + 1] = jnp.zeros(avg.shape[1:], jnp.float32)
    avg_halo[...] = jnp.zeros(avg_halo.shape, jnp.float32)

    has_up, has_down = my_y > 0, my_y < n_gy - 1
    has_left, has_right = my_x > 0, my_x < n_gx - 1
    up, down = (jnp.maximum(my_y - 1, 0), my_x), (jnp.minimum(my_y + 1, n_gy - 1), my_x)
    left, right = (my_y, jnp.maximum(my_x - 1, 0)), (my_y, jnp.minimum(my_x + 1, n_gx - 1))

    barrier = pltpu.get_barrier_semaphore()
    for step in range(1, n_gx):
        pl.semaphore_signal(
            barrier, inc=1, device_id=(my_y, lax.rem(my_x + step, n_gx)), device_id_type=MESH
        )
    for present, device in ((has_up, up), (has_down, down)):

        @pl.when(present)
        def _(device=device):
            pl.semaphore_signal(barrier, inc=1, device_id=device, device_id_type=MESH)

    peers = n_gx - 1 + jnp.where(has_up, 1, 0) + jnp.where(has_down, 1, 0)
    pl.semaphore_wait(barrier, peers)

    def to_peer(step, source, target, send, recv):
        return pltpu.make_async_remote_copy(
            src_ref=source,
            dst_ref=target,
            send_sem=send.at[step],
            recv_sem=recv.at[step],
            device_id=(my_y, lax.rem(my_x + step, n_gx)),
            device_id_type=MESH,
        )

    own = pltpu.make_async_copy(wide_columns, table.at[my_x], own_sem)
    own.start()
    copies = [
        to_peer(step, wide_columns, table.at[my_x], table_send, table_recv)
        for step in range(1, n_gx)
    ]
    for copy in copies:
        copy.start()
    own.wait()
    for copy in copies:
        copy.wait()

    half = height // 2
    group = lax.broadcasted_iota(jnp.int32, (1, LANES), 1) // BRICK
    turns = []
    for d in range(n_gx):
        rank = jnp.zeros((1, LANES), jnp.int32)
        plane = jnp.zeros((1, LANES), jnp.int32)
        for p in range(columns.shape[0]):
            match = table[d, pl.ds(p, 1)] == my_x
            plane = jnp.where(match & (rank == group % 2), p, plane)
            rank = rank + jnp.where(match, 1, 0)
        turns.append((group - plane + 4) % 4)
    for d in range(n_gx):
        turn_table[pl.ds(d, 1)] = turns[d]

    pack_lane = lax.broadcasted_iota(jnp.int32, (across, LANES), 1)

    def rolled(x):
        return [x] + [pltpu.roll(x, k * BRICK, 1) for k in range(1, 4)]

    def pack(r, carry):
        low, high = rolled(second[r]), rolled(second[r + half])
        mixed = [jnp.where(pack_lane < LANES // 2, a, b) for a, b in zip(low, high)]
        for d in range(n_gx):
            turn = jnp.broadcast_to(turn_table[pl.ds(d, 1)], (across, LANES))
            value = jnp.where(turn == 0, mixed[0], mixed[1])
            value = jnp.where(turn == 2, mixed[2], value)
            packed[d, r] = jnp.where(turn == 3, mixed[3], value)
        return carry

    lax.fori_loop(0, half, pack, 0)
    copies = [
        to_peer(
            step,
            packed.at[lax.rem(my_x + step, n_gx)],
            gathered.at[my_x],
            gather_send,
            gather_recv,
        )
        for step in sorted(range(1, n_gx), key=lambda k: abs(k - n_gx // 2))
    ]
    for copy in copies:
        copy.start()
    own = pltpu.make_async_copy(packed.at[my_x], gathered.at[my_x], own_sem)
    own.start()
    own.wait()
    for copy in copies:
        copy.wait()

    lane = lax.broadcasted_iota(jnp.int32, (8, LANES), 1)
    sub = lax.broadcasted_iota(jnp.int32, (8, LANES), 0)

    def ones(condition):
        return jnp.where(condition, 1.0, 0.0).astype(jnp.float32)

    def flag(condition):
        return jnp.where(condition, 1.0, 0.0).astype(jnp.float32)

    bricks = columns.shape[0]
    picks = [columns[p] for p in range(bricks)]
    row_lane = pack_lane // BRICK
    seconds = []
    for p in range(bricks):
        before = jnp.zeros((across, LANES), jnp.int32)
        for q in range(p):
            before = before + jnp.where(picks[p] == picks[q], 1, 0)
        seconds.append(before)

    def make_average(r, carry):
        values = [None, None]
        for p in range(bricks):
            turned = rolled(gathered[picks[p], r])
            for k in range(2):
                at = p - 2 * k
                brick = jnp.where(seconds[p] > 0, turned[(at - 1) % 4], turned[at % 4])
                values[k] = brick if p == 0 else jnp.where(row_lane == p, brick, values[k])
        for k in range(2):
            row = r + k * half
            value = 0.5 * (first[row] + values[k])
            avg[row + 1, pl.ds(PAD, across)] = value
            avg_stage[0, pl.ds(row, 1)] = value[0:1]
            avg_stage[1, pl.ds(row, 1)] = value[across - 1 : across]
        return carry

    lax.fori_loop(0, half, make_average, 0)

    def remote(source, target, send, recv, device):
        return pltpu.make_async_remote_copy(
            src_ref=source,
            dst_ref=target,
            send_sem=send,
            recv_sem=recv,
            device_id=device,
            device_id_type=MESH,
        )

    def start_all(parts):
        for present, copy, _ in parts:

            @pl.when(present)
            def _(copy=copy):
                copy.start()

    def wait_all(parts):
        for present, copy, opposite in parts:

            @pl.when(present)
            def _(copy=copy, opposite=opposite):
                copy.wait_send()
                opposite.wait_recv()

    to_left = remote(avg_stage.at[0], avg_halo.at[1], avg_send.at[0], avg_recv.at[0], left)
    to_right = remote(avg_stage.at[1], avg_halo.at[0], avg_send.at[1], avg_recv.at[1], right)
    parts = [(has_left, to_left, to_right), (has_right, to_right, to_left)]
    start_all(parts)
    wait_all(parts)

    def place_average(r, carry):
        avg[r + 1, pl.ds(PAD - 1, 1)] = avg_halo[0, pl.ds(r, 1)]
        avg[r + 1, pl.ds(PAD + across, 1)] = avg_halo[1, pl.ds(r, 1)]
        return carry

    lax.fori_loop(0, height, place_average, 0)
    to_up = remote(avg.at[1], avg.at[height + 1], avg_send.at[2], avg_recv.at[2], up)
    to_down = remote(avg.at[height], avg.at[0], avg_send.at[3], avg_recv.at[3], down)
    parts = [(has_up, to_up, to_down), (has_down, to_down, to_up)]
    start_all(parts)
    wait_all(parts)

    def row_flags(l, r):
        h = hs[l]
        at = my_y * h + r
        return flag(at > 0), flag(at < n_gy * h - 1)

    def masks_of(l):
        w, planes = ws[l], LANES >> l
        first_column = ones((sub > 0) | has_left)
        last_column = ones((sub != (w - 1) % 8) | has_right)
        below = ones((lane > 0) & (lane < planes))
        above = ones(lane < planes - 1)
        return first_column, last_column, below, above

    masks = [masks_of(l) for l in range(LEVELS)]

    def exchange(l, b):
        h, wq = hs[l], wqs[l]
        u, stage, halo = iterates[l], stages[l], halos[l]
        base = bases[l] + 4 * b
        inner = pl.ds(PAD, wq)
        send = [halo_send.at[base + d] for d in range(4)]
        recv = [halo_recv.at[base + d] for d in range(4)]
        to_up = remote(u.at[b, :, 1, inner], u.at[b, :, h + 1, inner], send[0], recv[0], up)
        to_down = remote(u.at[b, :, h, inner], u.at[b, :, 0, inner], send[1], recv[1], down)
        to_left = remote(stage.at[b, 0], halo.at[b, 1], send[2], recv[2], left)
        to_right = remote(stage.at[b, 1], halo.at[b, 0], send[3], recv[3], right)
        return [
            (has_up, to_up, to_down),
            (has_down, to_down, to_up),
            (has_left, to_left, to_right),
            (has_right, to_right, to_left),
        ]

    def place_halo(l, b, r):
        u, halo, w = iterates[l], halos[l], ws[l]
        for i in range(3):
            u[b, i, r + 1, pl.ds(PAD - 1, 1)] = halo[b, 0, i, pl.ds(r, 1)]
            u[b, i, r + 1, pl.ds(PAD + w, 1)] = halo[b, 1, i, pl.ds(r, 1)]

    def store_chunk(l, b, r, j, new):
        u, stage, w = iterates[l], stages[l], ws[l]
        for i in range(3):
            u[b, i, r + 1, pl.ds(PAD + 8 * j, 8)] = new[i]
            if b < EXCHANGES[l]:
                if j == 0:
                    stage[b, 0, i, pl.ds(r, 1)] = new[i][0:1]
                if j == wqs[l] // 8 - 1:
                    k = (w - 1) % 8
                    stage[b, 1, i, pl.ds(r, 1)] = new[i][k : k + 1]

    def faces(l, b, r, j, flags):
        u = iterates[l]
        s = PAD + 8 * j
        scale = 0.25**l / (CONTRAST * CONTRAST)
        first_column, last_column, below, above = masks[l]
        center = [u[b, i, r + 1, pl.ds(s, 8)] for i in range(3)]
        sides = [
            ([u[b, i, r, pl.ds(s, 8)] for i in range(3)], flags[0]),
            ([u[b, i, r + 2, pl.ds(s, 8)] for i in range(3)], flags[1]),
            (
                [u[b, i, r + 1, pl.ds(s - 1, 8)] for i in range(3)],
                first_column if j == 0 else None,
            ),
            (
                [u[b, i, r + 1, pl.ds(s + 1, 8)] for i in range(3)],
                last_column if j == wqs[l] // 8 - 1 else None,
            ),
            ([pltpu.roll(c, 1, 1) for c in center], below),
            ([pltpu.roll(c, LANES - 1, 1) for c in center], above),
        ]
        total, weighted = None, None
        for values, mask in sides:
            change = [v - c for v, c in zip(values, center)]
            spread = change[0] * change[0] + change[1] * change[1] + change[2] * change[2]
            weight = lax.rsqrt(1.0 + spread * scale)
            if mask is not None:
                weight = weight * mask
            terms = [weight * v for v in values]
            total = weight if total is None else total + weight
            weighted = terms if weighted is None else [a + t for a, t in zip(weighted, terms)]
        return center, weighted, total

    def row_loop(l, work):
        def step(r, carry):
            work(r)
            return carry

        lax.fori_loop(0, hs[l], step, 0)

    def grouped_loop(l, work):
        group = min(4, hs[l])

        def step(r, carry):
            for k in range(group):
                work(r * group + k)
            return carry

        lax.fori_loop(0, hs[l] // group, step, 0)

    def tensor_of(l, r, j):
        return [tensors[l][k, r, pl.ds(8 * j, 8)] for k in range(6)]

    def source_of(l, r, j):
        return [sources[l][k, r, pl.ds(8 * j, 8)] for k in range(3)]

    def relaxed(l, center, weighted, total, tensor, source):
        coupling = 0.25**l
        solved = solve_three(
            tensor,
            TIKHONOV + coupling * total,
            [f + coupling * q for f, q in zip(source, weighted)],
        )
        return [c + RELAXATION * (s - c) for c, s in zip(center, solved)]

    def applied(l, center, weighted, total, tensor):
        coupling = 0.25**l
        return [
            a + TIKHONOV * c + coupling * (total * c - q)
            for a, c, q in zip(apply_three(tensor, center), center, weighted)
        ]

    def chunk_loop(l, b, compute, store):
        chunks = wqs[l] // 8
        group = min(hs[l], max(1, 4 // chunks))

        def step(at, carry):
            rows = [at * group + k for k in range(group)]
            for r in rows:
                place_halo(l, b, r)
            results = []
            for r in rows:
                flags = row_flags(l, r)
                for j in range(chunks):
                    results.append((r, j, compute(r, j, flags)))
            for r, j, result in results:
                store(r, j, result)
            return carry

        lax.fori_loop(0, hs[l] // group, step, 0)

    def relax(l, b, target):
        def compute(r, j, flags):
            center, weighted, total = faces(l, b, r, j, flags)
            return relaxed(l, center, weighted, total, tensor_of(l, r, j), source_of(l, r, j))

        def store(r, j, new):
            if target is None:
                for i in range(3):
                    out[i, r, pl.ds(8 * j, 8)] = new[i]
            else:
                store_chunk(l, target, r, j, new)

        chunk_loop(l, b, compute, store)

    def residue(l, b):
        def compute(r, j, flags):
            center, weighted, total = faces(l, b, r, j, flags)
            value = applied(l, center, weighted, total, tensor_of(l, r, j))
            return [f - v for f, v in zip(source_of(l, r, j), value)]

        def store(r, j, new):
            for i in range(3):
                residues[l][i, r, pl.ds(8 * j, 8)] = new[i]

        chunk_loop(l, b, compute, store)

    def enter(l):
        def compute(r, j, flags):
            center, weighted, total = faces(l, 0, r, j, flags)
            tensor = tensor_of(l, r, j)
            value = applied(l, center, weighted, total, tensor)
            source = [f + v for f, v in zip(source_of(l, r, j), value)]
            return source, relaxed(l, center, weighted, total, tensor, source)

        def store(r, j, result):
            source, new = result
            for i in range(3):
                sources[l][i, r, pl.ds(8 * j, 8)] = source[i]
            store_chunk(l, 1, r, j, new)

        chunk_loop(l, 0, compute, store)

    def pair_matrix(rows, cols, fine_of, blocks):
        fine, coarse, coarse_padded = blocks
        i = lax.broadcasted_iota(jnp.int32, (rows, cols), 0)
        j = lax.broadcasted_iota(jnp.int32, (rows, cols), 1)
        f, c = (j, i) if fine_of == 1 else (i, j)
        return ones(
            (f // fine == c // coarse_padded)
            & ((f % fine) // 2 == c % coarse_padded)
            & (c % coarse_padded < coarse)
        )

    def doubled(matrix, axis):
        return jnp.concatenate([matrix, matrix], axis=axis).astype(jnp.bfloat16)

    lane_blocks = (LANES, LANES // 2, LANES)

    def shrink(l, count, fine_row, store):
        w, wc = wqs[l], wqs[l + 1]
        blocks = (w, ws[l + 1], wc)
        squeeze = doubled(pair_matrix(LANES, LANES, 0, lane_blocks), 0)
        join = doubled(pair_matrix(count * wc, count * w, 1, blocks), 1)

        def work(r):
            x = (fine_row(2 * r) + fine_row(2 * r + 1)).reshape(count * w, LANES)
            y = dot(join, two_terms(dot(two_terms(x, 1), squeeze), 0)) * 0.125
            store(r, y.reshape(count, wc, LANES))

        grouped_loop(l + 1, work)

    def shrink_iterate(l, b):
        u = iterates[l]
        coarse, stage, wc = iterates[l + 1], stages[l + 1], ws[l + 1]

        def store(r, y):
            coarse[0, :, r + 1, pl.ds(PAD, wqs[l + 1])] = y
            for i in range(3):
                stage[0, 0, i, pl.ds(r, 1)] = y[i, 0:1]
                stage[0, 1, i, pl.ds(r, 1)] = y[i, wc - 1 : wc]

        shrink(l, 3, lambda r: u[b, :, r + 1, pl.ds(PAD, wqs[l])], store)

    def shrink_array(l, count, fine, coarse):
        def store(r, y):
            coarse[:, r] = y

        shrink(l, count, lambda r: fine[:, r], store)

    def grow(l, b, solved, target):
        w, wc = wqs[l], wqs[l + 1]
        u, coarse, stage = iterates[l], iterates[l + 1], stages[l]
        spread = doubled(pair_matrix(LANES, LANES, 1, lane_blocks), 0)
        split = doubled(pair_matrix(3 * w, 3 * wc, 0, (w, ws[l + 1], wc)), 1)

        def work(r):
            inner = pl.ds(PAD, wc)
            if ws[l + 1] < wc:
                kept = lax.broadcasted_iota(jnp.int32, (3, wc, LANES), 1) < ws[l + 1]
                x = jnp.where(kept, coarse[solved, :, r + 1, inner] - coarse[0, :, r + 1, inner], 0.0)
            else:
                x = coarse[solved, :, r + 1, inner] - coarse[0, :, r + 1, inner]
            y = dot(two_terms(x.reshape(3 * wc, LANES), 1), spread)
            y = dot(split, two_terms(y, 0)).reshape(3, w, LANES)
            for row in range(2):
                at = 2 * r + row
                new = u[b, :, at + 1, pl.ds(PAD, w)] + y
                u[target, :, at + 1, pl.ds(PAD, w)] = new
                for i in range(3):
                    stage[target, 0, i, pl.ds(at, 1)] = new[i, 0:1]
                    stage[target, 1, i, pl.ds(at, 1)] = new[i, ws[l] - 1 : ws[l]]

        grouped_loop(l + 1, work)

    first_column, last_column, below, above = masks[0]

    def motion(r):
        flags = row_flags(0, r)
        for j in range(across // 8):
            s = PAD + 8 * j
            diffs, sums = [], []
            for shift in (-1, 0, 1):
                lower = avg[r, pl.ds(s + shift, 8)]
                middle = avg[r + 1, pl.ds(s + shift, 8)]
                upper = avg[r + 2, pl.ds(s + shift, 8)]
                diffs.append(0.5 * (upper - lower))
                sums.append(0.25 * (lower + 2.0 * middle + upper))
            along_rows = 0.25 * (diffs[0] + 2.0 * diffs[1] + diffs[2])
            along_cols = 0.5 * (sums[2] - sums[0])
            along_planes = 0.25 * (sums[0] + 2.0 * sums[1] + sums[2])

            def beside(x):
                return pltpu.roll(x, 1, 1) * below, pltpu.roll(x, LANES - 1, 1) * above

            def smooth(x):
                lower, upper = beside(x)
                return 0.25 * (lower + 2.0 * x + upper)

            g0, g1 = smooth(along_rows), smooth(along_cols)
            lower, upper = beside(along_planes)
            g2 = 0.5 * (upper - lower)
            normal = 1.0 / (g0 * g0 + g1 * g1 + g2 * g2 + FLOOR)
            n0, n1, n2 = g0 * normal, g1 * normal, g2 * normal
            tensor = [n0 * g0, n0 * g1, n0 * g2, n1 * g1, n1 * g2, n2 * g2]
            base = first[r, pl.ds(8 * j, 8)]
            temporal = 2.0 * (avg[r + 1, pl.ds(s, 8)] - base)
            source = [-n0 * temporal, -n1 * temporal, -n2 * temporal]
            for k in range(6):
                tensors[0][k, r, pl.ds(8 * j, 8)] = tensor[k]
            for k in range(3):
                sources[0][k, r, pl.ds(8 * j, 8)] = source[k]
            total = below + above + (flags[0] + flags[1])
            total = total + (first_column if j == 0 else 1.0)
            total = total + (last_column if j == across // 8 - 1 else 1.0)
            solved = solve_three(tensor, TIKHONOV + total, source)
            store_chunk(0, 0, r, j, [RELAXATION * x for x in solved])

    row_loop(0, motion)

    current = exchange(0, 0)
    start_all(current)
    for l in range(LEVELS - 1):
        shrink_array(l, 6, tensors[l], tensors[l + 1])
    wait_all(current)
    relax(0, 0, 1)
    for l in range(LEVELS - 1):
        b = 1 if l == 0 else 2
        current = exchange(l, b)
        start_all(current)
        shrink_iterate(l, b)
        following = exchange(l + 1, 0)
        start_all(following)
        wait_all(current)
        residue(l, b)
        shrink_array(l, 3, residues[l], sources[l + 1])
        wait_all(following)
        enter(l + 1)
        current = exchange(l + 1, 1)
        start_all(current)
        wait_all(current)
        relax(l + 1, 1, 2)
    for l in range(LEVELS - 2, -1, -1):
        b = 1 if l == 0 else 2
        grow(l, b, 2 if l == LEVELS - 2 else 5, b + 1)
        for sweep in range(2):
            current = exchange(l, b + 1 + sweep)
            start_all(current)
            wait_all(current)
            last = l == 0 and sweep == 1
            relax(l, b + 1 + sweep, None if last else b + 2 + sweep)


def body(n_gy, n_gx, first_frame, second_frame, source_column):
    height, across, planes = first_frame.shape
    f32 = jnp.float32
    hs = [height >> l for l in range(LEVELS)]
    wqs = [max(across >> l, 8) for l in range(LEVELS)]
    hqs = [max(h, 8) for h in hs]
    total = sum(EXCHANGES) * 4
    vmem = pl.BlockSpec(memory_space=pltpu.VMEM)
    scratch = [
        pltpu.VMEM((n_gx, height // 2, across, LANES), f32),
        pltpu.VMEM((height + 2, across + 2 * PAD, LANES), f32),
        pltpu.VMEM((2, height, LANES), f32),
        pltpu.VMEM((2, height, LANES), f32),
    ]
    scratch += [pltpu.VMEM((6, hs[l], wqs[l], LANES), f32) for l in range(LEVELS)]
    scratch += [pltpu.VMEM((3, hs[l], wqs[l], LANES), f32) for l in range(LEVELS)]
    scratch += [
        pltpu.VMEM((BUFFERS[l], 3, hs[l] + 2, wqs[l] + 2 * PAD, LANES), f32)
        for l in range(LEVELS)
    ]
    scratch += [pltpu.VMEM((EXCHANGES[l], 2, 3, hqs[l], LANES), f32) for l in range(LEVELS)] * 2
    scratch += [pltpu.VMEM((3, hs[l], wqs[l], LANES), f32) for l in range(LEVELS - 1)]
    dma = pltpu.SemaphoreType.DMA
    scratch += [dma((n_gx,)), dma((n_gx,)), dma((total,)), dma((total,)), dma((4,)), dma((4,)), dma]
    scratch += [
        pltpu.VMEM((n_gx, height // 2, across, LANES), f32),
        pltpu.VMEM((n_gx, 8, LANES), jnp.int32),
        pltpu.VMEM((n_gx, LANES), jnp.int32),
        dma((n_gx,)),
        dma((n_gx,)),
    ]
    columns = source_column.reshape(-1)
    wide = jnp.broadcast_to(jnp.pad(columns, (0, 8 - columns.shape[0]))[:, None], (8, LANES))
    return pl.pallas_call(
        functools.partial(kernel, n_gy, n_gx, height, across),
        out_shape=jax.ShapeDtypeStruct((3, height, across, planes), f32),
        in_specs=[vmem, vmem, pl.BlockSpec(memory_space=pltpu.SMEM), vmem],
        out_specs=vmem,
        scratch_shapes=scratch,
        compiler_params=pltpu.CompilerParams(
            collective_id=0, has_side_effects=True, vmem_limit_bytes=56 * 1024 * 1024
        ),
    )(first_frame, second_frame, columns, wide)


def solution(mesh):
    return jax.shard_map(
        functools.partial(body, mesh.shape["gy"], mesh.shape["gx"]),
        mesh=mesh,
        in_specs=(P("gy", "gx", None), P("gy", "gx", None), P("gy", "gx", None, None)),
        out_specs=P(None, "gy", "gx", None),
        check_vma=False,
    )
```

profile of v0, /device:TPU:0, one launch (start us, length us, event | category | flops | bytes accessed | tf_op | source)
XLA Modules:
  0.0 155.3 jit_solution(15198022838694429652)
XLA Ops:
  0.0 0.7 pad.4
  0.7 0.7 broadcast_in_dim.2.refs_3_
  1.3 151.3 %shard_map.37 = f32[3,32,32,128]{3,2,1,0:T(8,128)} custom-call(f32[32,32,128]{2,1,0:T(8,128)} %refs_0_.1, f32[32,32,128]{2,1,0:T(8,128)} %refs_1_.1, s32[4]{0:T(128)} %bitcast.2, s32[8,128]{1,0:T(8,128)} %broadcast_in_dim.2.refs_3_), custom_call_target="tpu_custom_call" | custom-call | tf_op jit(solution)/shard_map/pallas_call | solution.py:623
  152.6 2.7 %copy.5 = f32[3,32,32,128]{3,2,1,0:T(8,128)} copy(f32[3,32,32,128]{3,2,1,0:T(8,128)} %shard_map.37) | data formatting | bytes 3145728
where the time goes:
time: 155 us
  Pallas kernels  151 us (97%)
  local copies, waits for them, and re-layouts  3.99 us (3%)
    pallas_call x1, Pallas kernels, body(): pl.pallas_call(functools.partial(kernel, n_gy, n_gx, height, across), out...  151 us

commit v1 on v0

--- a/solution.py
+++ b/solution.py
@@ -15,6 +15,8 @@
 FLOOR = 1.0
 LANES = 128
 PAD = 8
+ROWS = 4
+LAYERS = 4
 BUFFERS = (4, 6, 6, 3)
 EXCHANGES = (4, 5, 5, 2)
 MESH = pl.DeviceIdType.MESH
@@ -57,17 +59,18 @@
 
 
 def kernel(n_gy, n_gx, height, across, *refs):
-    first, second, columns, wide_columns, out = refs[:5]
-    refs = refs[1:]
-    gathered, avg, avg_stage, avg_halo = refs[4:8]
+    first, second, columns, out = refs[:4]
+    cols, packets_in, packets_out, avg, avg_stage, avg_halo = refs[4:10]
+    refs = refs[2:]
     tensors = refs[8:12]
     sources = refs[12:16]
     iterates = refs[16:20]
     stages = refs[20:24]
     halos = refs[24:28]
     residues = refs[28:31]
-    gather_send, gather_recv, halo_send, halo_recv, avg_send, avg_recv, own_sem = refs[31:38]
-    packed, table, turn_table, table_send, table_recv = refs[38:]
+    halo_send, halo_recv, avg_send, avg_recv, own_sem = refs[31:36]
+    mine, table, picks, table_send, table_recv = refs[36:41]
+    own_send, packet_send, col_recv, packet_recv, edge_send, edge_recv = refs[41:]
     my_y, my_x = lax.axis_index("gy"), lax.axis_index("gx")
     bases = [sum(EXCHANGES[:l]) * 4 for l in range(LEVELS)]
     hs = [height >> l for l in range(LEVELS)]
@@ -115,102 +118,17 @@
             device_id_type=MESH,
         )
 
-    own = pltpu.make_async_copy(wide_columns, table.at[my_x], own_sem)
-    own.start()
-    copies = [
-        to_peer(step, wide_columns, table.at[my_x], table_send, table_recv)
-        for step in range(1, n_gx)
-    ]
-    for copy in copies:
-        copy.start()
-    own.wait()
-    for copy in copies:
-        copy.wait()
-
-    half = height // 2
-    group = lax.broadcasted_iota(jnp.int32, (1, LANES), 1) // BRICK
-    turns = []
-    for d in range(n_gx):
-        rank = jnp.zeros((1, LANES), jnp.int32)
-        plane = jnp.zeros((1, LANES), jnp.int32)
-        for p in range(columns.shape[0]):
-            match = table[d, pl.ds(p, 1)] == my_x
-            plane = jnp.where(match & (rank == group % 2), p, plane)
-            rank = rank + jnp.where(match, 1, 0)
-        turns.append((group - plane + 4) % 4)
-    for d in range(n_gx):
-        turn_table[pl.ds(d, 1)] = turns[d]
-
-    pack_lane = lax.broadcasted_iota(jnp.int32, (across, LANES), 1)
-
-    def rolled(x):
-        return [x] + [pltpu.roll(x, k * BRICK, 1) for k in range(1, 4)]
-
-    def pack(r, carry):
-        low, high = rolled(second[r]), rolled(second[r + half])
-        mixed = [jnp.where(pack_lane < LANES // 2, a, b) for a, b in zip(low, high)]
-        for d in range(n_gx):
-            turn = jnp.broadcast_to(turn_table[pl.ds(d, 1)], (across, LANES))
-            value = jnp.where(turn == 0, mixed[0], mixed[1])
-            value = jnp.where(turn == 2, mixed[2], value)
-            packed[d, r] = jnp.where(turn == 3, mixed[3], value)
-        return carry
-
-    lax.fori_loop(0, half, pack, 0)
-    copies = [
-        to_peer(
-            step,
-            packed.at[lax.rem(my_x + step, n_gx)],
-            gathered.at[my_x],
-            gather_send,
-            gather_recv,
-        )
-        for step in sorted(range(1, n_gx), key=lambda k: abs(k - n_gx // 2))
-    ]
-    for copy in copies:
-        copy.start()
-    own = pltpu.make_async_copy(packed.at[my_x], gathered.at[my_x], own_sem)
-    own.start()
-    own.wait()
-    for copy in copies:
-        copy.wait()
-
     lane = lax.broadcasted_iota(jnp.int32, (8, LANES), 1)
     sub = lax.broadcasted_iota(jnp.int32, (8, LANES), 0)
+    group = lax.broadcasted_iota(jnp.int32, (1, LANES), 1) // BRICK
+    bricks = columns.shape[0]
+    chunks = height // ROWS
 
     def ones(condition):
         return jnp.where(condition, 1.0, 0.0).astype(jnp.float32)
 
     def flag(condition):
         return jnp.where(condition, 1.0, 0.0).astype(jnp.float32)
-
-    bricks = columns.shape[0]
-    picks = [columns[p] for p in range(bricks)]
-    row_lane = pack_lane // BRICK
-    seconds = []
-    for p in range(bricks):
-        before = jnp.zeros((across, LANES), jnp.int32)
-        for q in range(p):
-            before = before + jnp.where(picks[p] == picks[q], 1, 0)
-        seconds.append(before)
-
-    def make_average(r, carry):
-        values = [None, None]
-        for p in range(bricks):
-            turned = rolled(gathered[picks[p], r])
-            for k in range(2):
-                at = p - 2 * k
-                brick = jnp.where(seconds[p] > 0, turned[(at - 1) % 4], turned[at % 4])
-                values[k] = brick if p == 0 else jnp.where(row_lane == p, brick, values[k])
-        for k in range(2):
-            row = r + k * half
-            value = 0.5 * (first[row] + values[k])
-            avg[row + 1, pl.ds(PAD, across)] = value
-            avg_stage[0, pl.ds(row, 1)] = value[0:1]
-            avg_stage[1, pl.ds(row, 1)] = value[across - 1 : across]
-        return carry
-
-    lax.fori_loop(0, half, make_average, 0)
 
     def remote(source, target, send, recv, device):
         return pltpu.make_async_remote_copy(
@@ -237,23 +155,210 @@
                 copy.wait_send()
                 opposite.wait_recv()
 
-    to_left = remote(avg_stage.at[0], avg_halo.at[1], avg_send.at[0], avg_recv.at[0], left)
-    to_right = remote(avg_stage.at[1], avg_halo.at[0], avg_send.at[1], avg_recv.at[1], right)
-    parts = [(has_left, to_left, to_right), (has_right, to_right, to_left)]
-    start_all(parts)
-    wait_all(parts)
-
-    def place_average(r, carry):
-        avg[r + 1, pl.ds(PAD - 1, 1)] = avg_halo[0, pl.ds(r, 1)]
-        avg[r + 1, pl.ds(PAD + across, 1)] = avg_halo[1, pl.ds(r, 1)]
+    def rows_of(c):
+        return pl.ds(c * ROWS, ROWS)
+
+    def chunk_copy(source, target, send, recv, device):
+        return remote(source, target, send, recv, device)
+
+    layered = n_gx == 2 * LAYERS
+    z, x = my_x // 2, my_x % 2
+    inner = (z > 0) & (z < LAYERS - 1)
+    ending = jnp.logical_not(inner)
+    near = jnp.where(z == 0, 1, jnp.where(z == LAYERS - 1, LAYERS - 2, LAYERS - 1 - z))
+    far = LAYERS - 1 - near
+    end = jnp.where(z <= 1, 0, LAYERS - 1)
+
+    def own_copies(c):
+        rows = second.at[rows_of(c)]
+        if not layered:
+            return [
+                (
+                    None,
+                    remote(
+                        rows,
+                        cols.at[my_x, rows_of(c)],
+                        own_send.at[step, c],
+                        col_recv.at[step, c],
+                        (my_y, lax.rem(my_x + step, n_gx)),
+                    ),
+                )
+                for step in range(1, n_gx)
+            ]
+        land = cols.at[z, rows_of(c)]
+        return [
+            (ending, remote(rows, land, own_send.at[1, c], col_recv.at[z, c], (my_y, 2 * far + x))),
+            (None, remote(rows, land, own_send.at[0, c], col_recv.at[z, c], (my_y, 2 * near + x))),
+            (ending, remote(rows, land, own_send.at[2, c], col_recv.at[z, c], (my_y, 2 * z + 1 - x))),
+        ]
+
+    def column_arrival(k, c):
+        return remote(
+            second.at[rows_of(c)],
+            cols.at[k, rows_of(c)],
+            own_send.at[0, c],
+            col_recv.at[k, c],
+            (my_y, lax.rem(my_x + 1, n_gx)),
+        )
+
+    def packet_copies(c):
+        targets = [(my_y, 2 * end), (my_y, 2 * end + 1), (my_y, 2 * z + 1 - x)]
+        return [
+            remote(
+                packets_out.at[i, rows_of(c)],
+                packets_in.at[x, rows_of(c)],
+                packet_send.at[i, c],
+                packet_recv.at[x, c],
+                device,
+            )
+            for i, device in enumerate(targets)
+        ]
+
+    def packet_arrival(k, c):
+        return remote(
+            packets_out.at[0, rows_of(c)],
+            packets_in.at[k, rows_of(c)],
+            packet_send.at[0, c],
+            packet_recv.at[k, c],
+            (my_y, lax.rem(my_x + 1, n_gx)),
+        )
+
+    def guarded(condition, act):
+        if condition is None:
+            act()
+        else:
+            pl.when(condition)(act)
+
+    def send_own(t, carry):
+        for condition, copy in own_copies((t + chunks - 1) % chunks):
+            guarded(condition, copy.start)
         return carry
 
-    lax.fori_loop(0, height, place_average, 0)
-    to_up = remote(avg.at[1], avg.at[height + 1], avg_send.at[2], avg_recv.at[2], up)
-    to_down = remote(avg.at[height], avg.at[0], avg_send.at[3], avg_recv.at[3], down)
-    parts = [(has_up, to_up, to_down), (has_down, to_down, to_up)]
-    start_all(parts)
-    wait_all(parts)
+    for p in range(8):
+        mine[pl.ds(p, 1)] = jnp.full((1, LANES), columns[min(p, bricks - 1)], jnp.int32)
+    if layered:
+        copies = [
+            to_peer(step, mine, table.at[my_x], table_send, table_recv) for step in range(1, n_gx)
+        ]
+        for copy in copies:
+            copy.start()
+        keep = pltpu.make_async_copy(second, cols.at[z], own_sem)
+        pl.when(inner)(keep.start)
+    lax.fori_loop(0, chunks, send_own, 0)
+
+    def wanted(entry):
+        value = entry(0)
+        for p in range(1, bricks):
+            value = jnp.where(group == p, entry(p), value)
+        return value
+
+    picks[pl.ds(3, 1)] = wanted(lambda p: mine[pl.ds(p, 1)])
+    if layered:
+        pl.when(inner)(keep.wait)
+        for copy in copies:
+            copy.wait()
+        for i, device in enumerate((2 * end, 2 * end + 1, 2 * z + 1 - x)):
+            picks[pl.ds(i, 1)] = wanted(lambda p: table[device, pl.ds(p, 1)])
+
+    def pick_of(i):
+        return jnp.broadcast_to(picks[pl.ds(i, 1)], (across, LANES))
+
+    def by_layer(values, layers):
+        value = values[0]
+        for k in range(1, LAYERS):
+            value = jnp.where(layers == k, values[k], value)
+        return value
+
+    def forward(c):
+        for k in range(LAYERS):
+
+            @pl.when(z != k)
+            def _(k=k):
+                column_arrival(k, c).wait_recv()
+
+        layers = [pick_of(i) // 2 for i in range(3)]
+        for row in range(ROWS):
+            r = c * ROWS + row
+            values = [cols[k, r] for k in range(LAYERS)]
+            for i in range(3):
+                packets_out[i, r] = by_layer(values, layers[i])
+        for copy in packet_copies(c):
+            copy.start()
+
+    def edges(c):
+        return [
+            (
+                has_left,
+                remote(avg_stage.at[c, 0], avg_halo.at[c, 1], edge_send.at[0, c], edge_recv.at[0, c], left),
+                remote(avg_stage.at[c, 1], avg_halo.at[c, 0], edge_send.at[1, c], edge_recv.at[1, c], right),
+            ),
+            (
+                has_right,
+                remote(avg_stage.at[c, 1], avg_halo.at[c, 0], edge_send.at[1, c], edge_recv.at[1, c], right),
+                remote(avg_stage.at[c, 0], avg_halo.at[c, 1], edge_send.at[0, c], edge_recv.at[0, c], left),
+            ),
+        ]
+
+    def average(c, row, value):
+        r = c * ROWS + row
+        value = 0.5 * (first[r] + value)
+        avg[r + 1, pl.ds(PAD, across)] = value
+        avg_stage[c, 0, pl.ds(row, 1)] = value[0:1]
+        avg_stage[c, 1, pl.ds(row, 1)] = value[across - 1 : across]
+
+    def averages(c):
+        pick = pick_of(3)
+        if not layered:
+            for step in range(1, n_gx):
+                remote(
+                    second.at[rows_of(c)],
+                    cols.at[lax.rem(my_x - step + n_gx, n_gx), rows_of(c)],
+                    own_send.at[step, c],
+                    col_recv.at[step, c],
+                    (my_y, lax.rem(my_x + step, n_gx)),
+                ).wait_recv()
+            for row in range(ROWS):
+                value = second[c * ROWS + row]
+                for step in range(1, n_gx):
+                    k = lax.rem(my_x + step, n_gx)
+                    value = jnp.where(pick == k, cols[k, c * ROWS + row], value)
+                average(c, row, value)
+        else:
+            layer, side = pick // 2, pick % 2
+
+            @pl.when(inner)
+            def _():
+                packet_arrival(1 - x, c).wait_recv()
+                for row in range(ROWS):
+                    r = c * ROWS + row
+                    value = by_layer([cols[k, r] for k in range(LAYERS)], layer)
+                    average(c, row, jnp.where(side == x, value, packets_in[1 - x, r]))
+
+            @pl.when(ending)
+            def _():
+                column_arrival(z, c).wait_recv()
+                for k in range(2):
+                    packet_arrival(k, c).wait_recv()
+                for row in range(ROWS):
+                    r = c * ROWS + row
+                    value = jnp.where(side == 0, packets_in[0, r], packets_in[1, r])
+                    same = jnp.where(side == x, second[r], cols[z, r])
+                    average(c, row, jnp.where(layer == z, same, value))
+
+        for present, copy, _ in edges(c):
+            pl.when(present)(copy.start)
+
+    def place_average(c):
+        for present, _, opposite in edges(c):
+            pl.when(present)(opposite.wait_recv)
+        for row in range(ROWS):
+            r = c * ROWS + row
+            avg[r + 1, pl.ds(PAD - 1, 1)] = avg_halo[c, 0, pl.ds(row, 1)]
+            avg[r + 1, pl.ds(PAD + across, 1)] = avg_halo[c, 1, pl.ds(row, 1)]
+
+    to_up = remote(avg.at[1], avg.at[height + 1], avg_send.at[0], avg_recv.at[0], up)
+    to_down = remote(avg.at[height], avg.at[0], avg_send.at[1], avg_recv.at[1], down)
+    row_parts = [(has_up, to_up, to_down), (has_down, to_down, to_up)]
 
     def row_flags(l, r):
         h = hs[l]
@@ -552,7 +657,45 @@
             solved = solve_three(tensor, TIKHONOV + total, source)
             store_chunk(0, 0, r, j, [RELAXATION * x for x in solved])
 
-    row_loop(0, motion)
+    def motion_block(m):
+        for row in range(ROWS):
+            motion(m * ROWS + row)
+
+    def gather_step(s, carry):
+        def chunk_at(t):
+            return (t + chunks - 1) % chunks
+
+        if layered:
+            pl.when(inner & (s < chunks))(lambda: forward(chunk_at(s)))
+        pl.when((s >= 1) & (s <= chunks))(lambda: averages(chunk_at(s - 1)))
+        pl.when(s >= 2)(lambda: place_average(chunk_at(s - 2)))
+        pl.when(s == 3)(lambda: start_all(row_parts))
+        pl.when(s >= 5)(lambda: motion_block(s - 4))
+
+        @pl.when(s == chunks)
+        def _():
+            wait_all(row_parts)
+            motion_block(0)
+            for row in range(1, ROWS):
+                motion(height - ROWS + row)
+
+        return carry
+
+    lax.fori_loop(0, chunks + 2, gather_step, 0)
+    motion_block(chunks - 2)
+    motion(height - ROWS)
+
+    def finish_sends(c, carry):
+        for condition, copy in own_copies(c):
+            guarded(condition, copy.wait_send)
+        if layered:
+            for copy in packet_copies(c):
+                pl.when(inner)(copy.wait_send)
+        for present, copy, _ in edges(c):
+            pl.when(present)(copy.wait_send)
+        return carry
+
+    lax.fori_loop(0, chunks, finish_sends, 0)
 
     current = exchange(0, 0)
     start_all(current)
@@ -595,11 +738,16 @@
     hqs = [max(h, 8) for h in hs]
     total = sum(EXCHANGES) * 4
     vmem = pl.BlockSpec(memory_space=pltpu.VMEM)
+    chunks = height // ROWS
+    layered = n_gx == 2 * LAYERS
+    volume = (height, across, LANES)
     scratch = [
-        pltpu.VMEM((n_gx, height // 2, across, LANES), f32),
+        pltpu.VMEM((LAYERS if layered else n_gx, *volume), f32),
+        pltpu.VMEM((2, *volume) if layered else (2, 8, LANES), f32),
+        pltpu.VMEM((3, *volume) if layered else (3, 8, LANES), f32),
         pltpu.VMEM((height + 2, across + 2 * PAD, LANES), f32),
-        pltpu.VMEM((2, height, LANES), f32),
-        pltpu.VMEM((2, height, LANES), f32),
+        pltpu.VMEM((chunks, 2, 8, LANES), f32),
+        pltpu.VMEM((chunks, 2, 8, LANES), f32),
     ]
     scratch += [pltpu.VMEM((6, hs[l], wqs[l], LANES), f32) for l in range(LEVELS)]
     scratch += [pltpu.VMEM((3, hs[l], wqs[l], LANES), f32) for l in range(LEVELS)]
@@ -610,26 +758,31 @@
     scratch += [pltpu.VMEM((EXCHANGES[l], 2, 3, hqs[l], LANES), f32) for l in range(LEVELS)] * 2
     scratch += [pltpu.VMEM((3, hs[l], wqs[l], LANES), f32) for l in range(LEVELS - 1)]
     dma = pltpu.SemaphoreType.DMA
-    scratch += [dma((n_gx,)), dma((n_gx,)), dma((total,)), dma((total,)), dma((4,)), dma((4,)), dma]
+    scratch += [dma((total,)), dma((total,)), dma((2,)), dma((2,)), dma]
     scratch += [
-        pltpu.VMEM((n_gx, height // 2, across, LANES), f32),
+        pltpu.VMEM((8, LANES), jnp.int32),
         pltpu.VMEM((n_gx, 8, LANES), jnp.int32),
-        pltpu.VMEM((n_gx, LANES), jnp.int32),
+        pltpu.VMEM((8, LANES), jnp.int32),
         dma((n_gx,)),
         dma((n_gx,)),
+        dma((3 if layered else n_gx, chunks)),
+        dma((3, chunks)),
+        dma((LAYERS if layered else n_gx, chunks)),
+        dma((2, chunks)),
+        dma((2, chunks)),
+        dma((2, chunks)),
     ]
     columns = source_column.reshape(-1)
-    wide = jnp.broadcast_to(jnp.pad(columns, (0, 8 - columns.shape[0]))[:, None], (8, LANES))
     return pl.pallas_call(
         functools.partial(kernel, n_gy, n_gx, height, across),
         out_shape=jax.ShapeDtypeStruct((3, height, across, planes), f32),
-        in_specs=[vmem, vmem, pl.BlockSpec(memory_space=pltpu.SMEM), vmem],
+        in_specs=[vmem, vmem, pl.BlockSpec(memory_space=pltpu.SMEM)],
         out_specs=vmem,
         scratch_shapes=scratch,
         compiler_params=pltpu.CompilerParams(
             collective_id=0, has_side_effects=True, vmem_limit_bytes=56 * 1024 * 1024
         ),
-    )(first_frame, second_frame, columns, wide)
+    )(first_frame, second_frame, columns)
 
 
 def solution(mesh):

time: 155 us -> 138 us (0.89)
  Pallas kernels: 151 us -> 135 us
    pallas_call x1, Pallas kernels: 151 us -> 135 us  [body(): pl.pallas_call(functools.partial(kernel, n_gy, n_gx, height, across), out...]
where the time goes in v1:
time: 138 us; the launch traced here: 137 us
  Pallas kernels  135 us (98%)
  local copies, waits for them, and re-layouts  2.67 us (2%)
    pallas_call x1, Pallas kernels, body(): pl.pallas_call(functools.partial(kernel, n_gy, n_gx, height, across), out...  135 us

profile of v1, /device:TPU:0, one launch (start us, length us, event | category | flops | bytes accessed | tf_op | source)
XLA Modules:
  0.0 137.4 jit_solution(15625958066011839215)
XLA Ops:
  0.0 134.7 %shard_map.37 = f32[3,32,32,128]{3,2,1,0:T(8,128)} custom-call(f32[32,32,128]{2,1,0:T(8,128)} %refs_0_.1, f32[32,32,128]{2,1,0:T(8,128)} %refs_1_.1, s32[4]{0:T(128)} %bitcast.1), custom_call_target="tpu_custom_call" | custom-call | tf_op jit(solution)/shard_map/pallas_call | solution.py:776
  134.7 2.7 %copy.5 = f32[3,32,32,128]{3,2,1,0:T(8,128)} copy(f32[3,32,32,128]{3,2,1,0:T(8,128)} %shard_map.37) | data formatting | bytes 3145728

commit v2 on v1

--- a/solution.py
+++ b/solution.py
@@ -18,7 +18,7 @@
 ROWS = 4
 LAYERS = 4
 BUFFERS = (4, 6, 6, 3)
-EXCHANGES = (4, 5, 5, 2)
+AHEAD = 2
 MESH = pl.DeviceIdType.MESH
 
 
@@ -62,8 +62,10 @@
     first, second, columns, out = refs[:4]
     cols, packets_in, packets_out, avg, avg_stage, avg_halo = refs[4:10]
     refs = refs[2:]
-    tensors = refs[8:12]
-    sources = refs[12:16]
+    moved = refs[8]
+    tensors = (None, *refs[9:12])
+    sources = (None, *refs[12:15])
+    refs = refs[:15] + (None,) + refs[15:]
     iterates = refs[16:20]
     stages = refs[20:24]
     halos = refs[24:28]
@@ -72,14 +74,14 @@
     mine, table, picks, table_send, table_recv = refs[36:41]
     own_send, packet_send, col_recv, packet_recv, edge_send, edge_recv = refs[41:]
     my_y, my_x = lax.axis_index("gy"), lax.axis_index("gx")
-    bases = [sum(EXCHANGES[:l]) * 4 for l in range(LEVELS)]
+    bases = [sum(BUFFERS[:l]) * 4 for l in range(LEVELS)]
     hs = [height >> l for l in range(LEVELS)]
     ws = [across >> l for l in range(LEVELS)]
     wqs = [max(w, 8) for w in ws]
 
     for l in range(LEVELS):
         u, w, wq, h = iterates[l], ws[l], wqs[l], hs[l]
-        for b in range(EXCHANGES[l]):
+        for b in range(BUFFERS[l]):
             zero_row = jnp.zeros((3, wq + 2 * PAD, LANES), jnp.float32)
             u[b, :, 0] = zero_row
             u[b, :, h + 1] = zero_row
@@ -244,7 +246,7 @@
             copy.start()
         keep = pltpu.make_async_copy(second, cols.at[z], own_sem)
         pl.when(inner)(keep.start)
-    lax.fori_loop(0, chunks, send_own, 0)
+    lax.fori_loop(0, AHEAD, send_own, 0)
 
     def wanted(entry):
         value = entry(0)
@@ -403,61 +405,93 @@
         u, stage, w = iterates[l], stages[l], ws[l]
         for i in range(3):
             u[b, i, r + 1, pl.ds(PAD + 8 * j, 8)] = new[i]
-            if b < EXCHANGES[l]:
-                if j == 0:
-                    stage[b, 0, i, pl.ds(r, 1)] = new[i][0:1]
-                if j == wqs[l] // 8 - 1:
-                    k = (w - 1) % 8
-                    stage[b, 1, i, pl.ds(r, 1)] = new[i][k : k + 1]
-
-    def faces(l, b, r, j, flags):
+            if j == 0:
+                stage[b, 0, i, pl.ds(r, 1)] = new[i][0:1]
+            if j == wqs[l] // 8 - 1:
+                k = (w - 1) % 8
+                stage[b, 1, i, pl.ds(r, 1)] = new[i][k : k + 1]
+
+    last_sub = sub == 7
+
+    def sweep(l, b, start, count, js, group, compute, store):
         u = iterates[l]
-        s = PAD + 8 * j
-        scale = 0.25**l / (CONTRAST * CONTRAST)
-        first_column, last_column, below, above = masks[l]
-        center = [u[b, i, r + 1, pl.ds(s, 8)] for i in range(3)]
-        sides = [
-            ([u[b, i, r, pl.ds(s, 8)] for i in range(3)], flags[0]),
-            ([u[b, i, r + 2, pl.ds(s, 8)] for i in range(3)], flags[1]),
-            (
-                [u[b, i, r + 1, pl.ds(s - 1, 8)] for i in range(3)],
-                first_column if j == 0 else None,
-            ),
-            (
-                [u[b, i, r + 1, pl.ds(s + 1, 8)] for i in range(3)],
-                last_column if j == wqs[l] // 8 - 1 else None,
-            ),
-            ([pltpu.roll(c, 1, 1) for c in center], below),
-            ([pltpu.roll(c, LANES - 1, 1) for c in center], above),
-        ]
-        total, weighted = None, None
-        for values, mask in sides:
-            change = [v - c for v, c in zip(values, center)]
+        first_column, last_column, _, above = masks[l]
+        end = wqs[l] // 8 - 1
+        scale = 0.25**l / (CONTRAST * CONTRAST) / (4.0 if l == 0 else 1.0)
+
+        def at(r, j, shift=0):
+            return [u[b, i, r + 1, pl.ds(PAD + 8 * j + shift, 8)] for i in range(3)]
+
+        def face(before, after, mask):
+            change = [q - p for p, q in zip(before, after)]
             spread = change[0] * change[0] + change[1] * change[1] + change[2] * change[2]
-            weight = lax.rsqrt(1.0 + spread * scale)
+            if scale != 1.0:
+                spread = spread * scale
+            weight = lax.rsqrt(1.0 + spread)
             if mask is not None:
                 weight = weight * mask
-            terms = [weight * v for v in values]
-            total = weight if total is None else total + weight
-            weighted = terms if weighted is None else [a + t for a, t in zip(weighted, terms)]
-        return center, weighted, total
-
-    def row_loop(l, work):
-        def step(r, carry):
-            work(r)
+            return [weight * c for c in change] + [weight]
+
+        def row(r, carry):
+            flags = row_flags(l, r)
+            results, lower, previous = [], [], None
+            for n, j in enumerate(js):
+                center = at(r, j)
+                down = face(center, at(r + 1, j), flags[1])
+                lower.append(down)
+                side = face(center, [pltpu.roll(c, LANES - 1, 1) for c in center], above)
+                right = face(center, at(r, j, 1), last_column if j == end else None)
+                if j - 1 in js:
+                    left = [
+                        pltpu.roll(jnp.where(last_sub, p, q), 1, 0) for p, q in zip(previous, right)
+                    ]
+                else:
+                    left = face(at(r, j, -1), center, first_column if j == 0 else None)
+                previous = right
+                back = [pltpu.roll(v, 1, 1) for v in side]
+                up = carry[n]
+                flux = [
+                    (down[i] - up[i]) + (side[i] - back[i]) + (right[i] - left[i]) for i in range(3)
+                ]
+                total = (down[3] + up[3]) + (side[3] + back[3]) + (right[3] + left[3])
+                results.append(compute(r, j, center, flux, total))
+            return results, lower
+
+        def step(k, carry):
+            base = start + k * group
+            if 0 in js or end in js:
+                for n in range(group):
+                    place_halo(l, b, base + n)
+            done = []
+            for n in range(group):
+                results, carry = row(base + n, carry)
+                done.append(results)
+            for n in range(group):
+                for j, result in zip(js, done[n]):
+                    store(base + n, j, result)
             return carry
 
-        lax.fori_loop(0, hs[l], step, 0)
-
-    def grouped_loop(l, work):
-        group = min(4, hs[l])
-
-        def step(r, carry):
-            for k in range(group):
-                work(r * group + k)
-            return carry
-
-        lax.fori_loop(0, hs[l] // group, step, 0)
+        flags = row_flags(l, start)
+        carry = [face(at(start - 1, j), at(start, j), flags[0]) for j in js]
+        if count == group:
+            step(0, carry)
+        else:
+            lax.fori_loop(0, count // group, step, carry)
+
+    def part(l, b, which, compute, store):
+        h = hs[l]
+        every = tuple(range(wqs[l] // 8))
+        if which == "all":
+            sweep(l, b, 0, h, every, min(h, max(1, 4 // len(every))), compute, store)
+        elif which == "edge":
+            sweep(l, b, 0, h, (every[0], every[-1]), 2, compute, store)
+            for r in (0, h - 1):
+                sweep(l, b, r, 1, every[1:-1], 1, compute, store)
+        else:
+            sweep(l, b, 1, h - 2, every[1:-1], 2, compute, store)
+
+    def motion_of(r, j):
+        return [moved[k, r, pl.ds(8 * j, 8)] for k in range(5)]
 
     def tensor_of(l, r, j):
         return [tensors[l][k, r, pl.ds(8 * j, 8)] for k in range(6)]
@@ -465,45 +499,32 @@
     def source_of(l, r, j):
         return [sources[l][k, r, pl.ds(8 * j, 8)] for k in range(3)]
 
-    def relaxed(l, center, weighted, total, tensor, source):
+    def relax(l, b, target, which="all"):
         coupling = 0.25**l
-        solved = solve_three(
-            tensor,
-            TIKHONOV + coupling * total,
-            [f + coupling * q for f, q in zip(source, weighted)],
-        )
-        return [c + RELAXATION * (s - c) for c, s in zip(center, solved)]
-
-    def applied(l, center, weighted, total, tensor):
-        coupling = 0.25**l
-        return [
-            a + TIKHONOV * c + coupling * (total * c - q)
-            for a, c, q in zip(apply_three(tensor, center), center, weighted)
-        ]
-
-    def chunk_loop(l, b, compute, store):
-        chunks = wqs[l] // 8
-        group = min(hs[l], max(1, 4 // chunks))
-
-        def step(at, carry):
-            rows = [at * group + k for k in range(group)]
-            for r in rows:
-                place_halo(l, b, r)
-            results = []
-            for r in rows:
-                flags = row_flags(l, r)
-                for j in range(chunks):
-                    results.append((r, j, compute(r, j, flags)))
-            for r, j, result in results:
-                store(r, j, result)
-            return carry
-
-        lax.fori_loop(0, hs[l] // group, step, 0)
-
-    def relax(l, b, target):
-        def compute(r, j, flags):
-            center, weighted, total = faces(l, b, r, j, flags)
-            return relaxed(l, center, weighted, total, tensor_of(l, r, j), source_of(l, r, j))
+        gain = 0.5 if target is None else 1.0
+
+        def compute(r, j, center, flux, total):
+            if l == 0:
+                h0, h1, h2, time, hh = motion_of(r, j)
+                around = [q + total * c for q, c in zip(flux, center)]
+                diagonal = TIKHONOV + total
+                widened = diagonal + hh
+                common = h0 * around[0] + h1 * around[1] + h2 * around[2] + diagonal * time
+                inverse = (gain * RELAXATION) / (diagonal * widened)
+                keep = gain * (1.0 - RELAXATION)
+                return [
+                    keep * c + (q * widened - g * common) * inverse
+                    for c, q, g in zip(center, around, (h0, h1, h2))
+                ]
+            solved = solve_three(
+                tensor_of(l, r, j),
+                TIKHONOV + coupling * total,
+                [
+                    f + coupling * (q + total * c)
+                    for f, q, c in zip(source_of(l, r, j), flux, center)
+                ],
+            )
+            return [c + RELAXATION * (s - c) for c, s in zip(center, solved)]
 
         def store(r, j, new):
             if target is None:
@@ -512,27 +533,42 @@
             else:
                 store_chunk(l, target, r, j, new)
 
-        chunk_loop(l, b, compute, store)
-
-    def residue(l, b):
-        def compute(r, j, flags):
-            center, weighted, total = faces(l, b, r, j, flags)
-            value = applied(l, center, weighted, total, tensor_of(l, r, j))
-            return [f - v for f, v in zip(source_of(l, r, j), value)]
+        part(l, b, which, compute, store)
+
+    def residue(l, b, which="all"):
+        coupling = 0.25**l
+
+        def compute(r, j, center, flux, total):
+            if l == 0:
+                h0, h1, h2, time, _ = motion_of(r, j)
+                common = h0 * center[0] + h1 * center[1] + h2 * center[2] + time
+                return [
+                    q - TIKHONOV * c - g * common for c, q, g in zip(center, flux, (h0, h1, h2))
+                ]
+            value = apply_three(tensor_of(l, r, j), center)
+            return [
+                f + coupling * q - TIKHONOV * c - a
+                for f, q, c, a in zip(source_of(l, r, j), flux, center, value)
+            ]
 
         def store(r, j, new):
             for i in range(3):
                 residues[l][i, r, pl.ds(8 * j, 8)] = new[i]
 
-        chunk_loop(l, b, compute, store)
+        part(l, b, which, compute, store)
 
     def enter(l):
-        def compute(r, j, flags):
-            center, weighted, total = faces(l, 0, r, j, flags)
-            tensor = tensor_of(l, r, j)
-            value = applied(l, center, weighted, total, tensor)
-            source = [f + v for f, v in zip(source_of(l, r, j), value)]
-            return source, relaxed(l, center, weighted, total, tensor, source)
+        coupling = 0.25**l
+
+        def compute(r, j, center, flux, total):
+            tensor, given = tensor_of(l, r, j), source_of(l, r, j)
+            value = apply_three(tensor, center)
+            source = [
+                f + a + TIKHONOV * c - coupling * q
+                for f, a, c, q in zip(given, value, center, flux)
+            ]
+            solved = solve_three(tensor, TIKHONOV + coupling * total, given)
+            return source, [c + RELAXATION * s for c, s in zip(center, solved)]
 
         def store(r, j, result):
             source, new = result
@@ -540,79 +576,148 @@
                 sources[l][i, r, pl.ds(8 * j, 8)] = source[i]
             store_chunk(l, 1, r, j, new)
 
-        chunk_loop(l, 0, compute, store)
-
-    def pair_matrix(rows, cols, fine_of, blocks):
-        fine, coarse, coarse_padded = blocks
-        i = lax.broadcasted_iota(jnp.int32, (rows, cols), 0)
-        j = lax.broadcasted_iota(jnp.int32, (rows, cols), 1)
-        f, c = (j, i) if fine_of == 1 else (i, j)
-        return ones(
-            (f // fine == c // coarse_padded)
-            & ((f % fine) // 2 == c % coarse_padded)
-            & (c % coarse_padded < coarse)
-        )
-
-    def doubled(matrix, axis):
-        return jnp.concatenate([matrix, matrix], axis=axis).astype(jnp.bfloat16)
-
-    lane_blocks = (LANES, LANES // 2, LANES)
-
-    def shrink(l, count, fine_row, store):
-        w, wc = wqs[l], wqs[l + 1]
-        blocks = (w, ws[l + 1], wc)
-        squeeze = doubled(pair_matrix(LANES, LANES, 0, lane_blocks), 0)
-        join = doubled(pair_matrix(count * wc, count * w, 1, blocks), 1)
-
-        def work(r):
-            x = (fine_row(2 * r) + fine_row(2 * r + 1)).reshape(count * w, LANES)
-            y = dot(join, two_terms(dot(two_terms(x, 1), squeeze), 0)) * 0.125
-            store(r, y.reshape(count, wc, LANES))
-
-        grouped_loop(l + 1, work)
+        part(l, 0, "all", compute, store)
+
+    fine_lane = lax.broadcasted_iota(jnp.int32, (LANES, LANES), 0)
+    coarse_lane = lax.broadcasted_iota(jnp.int32, (LANES, LANES), 1)
+    halving = ones(fine_lane // 2 == coarse_lane)
+    squeeze = jnp.concatenate([halving, halving], axis=0).astype(jnp.bfloat16)
+    doubling = ones(coarse_lane // 2 == fine_lane)
+    spread = jnp.concatenate([doubling, doubling], axis=0).astype(jnp.bfloat16)
+
+    def corners(j, k, rest):
+        return [
+            (row, pl.ds(rest + 16 * j + parity, k, stride=2)) for row in range(2) for parity in range(2)
+        ]
+
+    def filled(x):
+        if x.shape[0] == 8:
+            return x
+        return jnp.concatenate([x, jnp.zeros((8 - x.shape[0], LANES), jnp.float32)], axis=0)
+
+    def shrink(l, rows, sums, factor, store):
+        chunks = wqs[l + 1] // 8
+        pieces = [[sums(r, j) for j in range(chunks)] for r in rows]
+        flat = [filled(x) for of_row in pieces for of_chunk in of_row for x in of_chunk]
+        y = dot(two_terms(jnp.concatenate(flat, axis=0), 1), squeeze) * factor
+        at = 0
+        for r in rows:
+            for j in range(chunks):
+                for i in range(len(pieces[0][0])):
+                    store(r, j, i, y[8 * at : 8 * at + 8])
+                    at += 1
+
+    def summed(load, cells):
+        values = [load(row, columns) for row, columns in cells]
+        return (values[0] + values[1]) + (values[2] + values[3])
+
+    def all_rows(l, work):
+        group = min(4, hs[l])
+
+        def step(k, carry):
+            work([k * group + n for n in range(group)])
+            return carry
+
+        if hs[l] == group:
+            step(0, 0)
+        else:
+            lax.fori_loop(0, hs[l] // group, step, 0)
 
     def shrink_iterate(l, b):
         u = iterates[l]
-        coarse, stage, wc = iterates[l + 1], stages[l + 1], ws[l + 1]
-
-        def store(r, y):
-            coarse[0, :, r + 1, pl.ds(PAD, wqs[l + 1])] = y
+        coarse, stage, w = iterates[l + 1], stages[l + 1], ws[l + 1]
+        k = min(8, w)
+
+        def sums(r, j):
+            cells = corners(j, k, PAD)
+            return [
+                summed(lambda row, columns, i=i: u[b, i, 2 * r + row + 1, columns], cells)
+                for i in range(3)
+            ]
+
+        def store(r, j, i, y):
+            coarse[0, i, r + 1, pl.ds(PAD + 8 * j, 8)] = y
+            if j == 0:
+                stage[0, 0, i, pl.ds(r, 1)] = y[0:1]
+            if j == wqs[l + 1] // 8 - 1:
+                n = (w - 1) % 8
+                stage[0, 1, i, pl.ds(r, 1)] = y[n : n + 1]
+
+        factor = 0.0625 if l == 0 else 0.125
+        all_rows(l + 1, lambda rows: shrink(l, rows, sums, factor, store))
+
+    def shrink_array(l, fine, coarse, factor):
+        k = min(8, ws[l + 1])
+
+        def sums(r, j):
+            cells = corners(j, k, 0)
+            return [
+                summed(lambda row, columns, i=i: fine[i, 2 * r + row, columns], cells)
+                for i in range(fine.shape[0])
+            ]
+
+        def store(r, j, i, y):
+            coarse[i, r, pl.ds(8 * j, 8)] = y
+
+        all_rows(l + 1, lambda rows: shrink(l, rows, sums, factor, store))
+
+    def shrink_motion(rows):
+        def sums(r, j):
+            values = None
+            for row, columns in corners(j, min(8, ws[1]), 0):
+                h0, h1, h2 = [moved[k, 2 * r + row, columns] for k in range(3)]
+                terms = [h0 * h0, h0 * h1, h0 * h2, h1 * h1, h1 * h2, h2 * h2]
+                values = terms if values is None else [v + t for v, t in zip(values, terms)]
+            return values
+
+        def store(r, j, i, y):
+            tensors[1][i, r, pl.ds(8 * j, 8)] = y
+
+        shrink(0, rows, sums, 0.125, store)
+
+    def grow(l, b, solved, target, arriving):
+        wc, hc, h = wqs[l + 1], hs[l + 1], hs[l]
+        kc, kr = min(8, ws[l + 1]), min(8, hc)
+        u, coarse = iterates[l], iterates[l + 1]
+
+        def spread_out(x):
+            y = dot(two_terms(x, 1), spread)
+            return 2.0 * y if l == 0 else y
+
+        def correction(r):
+            inner = pl.ds(PAD, wc)
+            return (coarse[solved, :, r + 1, inner] - coarse[0, :, r + 1, inner]).reshape(3 * wc, LANES)
+
+        def add(y, first_row, targets):
             for i in range(3):
-                stage[0, 0, i, pl.ds(r, 1)] = y[i, 0:1]
-                stage[0, 1, i, pl.ds(r, 1)] = y[i, wc - 1 : wc]
-
-        shrink(l, 3, lambda r: u[b, :, r + 1, pl.ds(PAD, wqs[l])], store)
-
-    def shrink_array(l, count, fine, coarse):
-        def store(r, y):
-            coarse[:, r] = y
-
-        shrink(l, count, lambda r: fine[:, r], store)
-
-    def grow(l, b, solved, target):
-        w, wc = wqs[l], wqs[l + 1]
-        u, coarse, stage = iterates[l], iterates[l + 1], stages[l]
-        spread = doubled(pair_matrix(LANES, LANES, 1, lane_blocks), 0)
-        split = doubled(pair_matrix(3 * w, 3 * wc, 0, (w, ws[l + 1], wc)), 1)
-
-        def work(r):
-            inner = pl.ds(PAD, wc)
-            if ws[l + 1] < wc:
-                kept = lax.broadcasted_iota(jnp.int32, (3, wc, LANES), 1) < ws[l + 1]
-                x = jnp.where(kept, coarse[solved, :, r + 1, inner] - coarse[0, :, r + 1, inner], 0.0)
-            else:
-                x = coarse[solved, :, r + 1, inner] - coarse[0, :, r + 1, inner]
-            y = dot(two_terms(x.reshape(3 * wc, LANES), 1), spread)
-            y = dot(split, two_terms(y, 0)).reshape(3, w, LANES)
-            for row in range(2):
-                at = 2 * r + row
-                new = u[b, :, at + 1, pl.ds(PAD, w)] + y
-                u[target, :, at + 1, pl.ds(PAD, w)] = new
-                for i in range(3):
-                    stage[target, 0, i, pl.ds(at, 1)] = new[i, 0:1]
-                    stage[target, 1, i, pl.ds(at, 1)] = new[i, ws[l] - 1 : ws[l]]
-
-        grouped_loop(l + 1, work)
+                for j in range(wc // 8):
+                    at = first_row + i * wc + 8 * j
+                    piece = y[at : at + kc]
+                    for row in targets:
+                        for parity in range(2):
+                            columns = pl.ds(PAD + 16 * j + parity, kc, stride=2)
+                            u[target, i, row, columns] = u[b, i, row, columns] + piece
+
+        def work(rows):
+            y = spread_out(jnp.concatenate([correction(r) for r in rows], axis=0))
+            for n, r in enumerate(rows):
+                add(y, n * 3 * wc, (2 * r + 1, 2 * r + 2))
+
+        all_rows(l + 1, work)
+        wait_all(arriving)
+        y = spread_out(jnp.concatenate([correction(-1), correction(hc)], axis=0))
+        add(y, 0, (0,))
+        add(y, 3 * wc, (h + 1,))
+        hq = max(8, hc)
+        halo, coarse_halo = halos[l], halos[l + 1]
+        y = spread_out((coarse_halo[solved] - coarse_halo[0]).reshape(6 * hq, LANES))
+        for side in range(2):
+            for i in range(3):
+                for j in range(hq // 8):
+                    at = (side * 3 + i) * hq + 8 * j
+                    for parity in range(2):
+                        rows = pl.ds(16 * j + parity, kr, stride=2)
+                        halo[target, side, i, rows] = halo[b, side, i, rows] + y[at : at + kr]
 
     first_column, last_column, below, above = masks[0]
 
@@ -641,27 +746,33 @@
             g0, g1 = smooth(along_rows), smooth(along_cols)
             lower, upper = beside(along_planes)
             g2 = 0.5 * (upper - lower)
-            normal = 1.0 / (g0 * g0 + g1 * g1 + g2 * g2 + FLOOR)
-            n0, n1, n2 = g0 * normal, g1 * normal, g2 * normal
-            tensor = [n0 * g0, n0 * g1, n0 * g2, n1 * g1, n1 * g2, n2 * g2]
+            square = g0 * g0 + g1 * g1 + g2 * g2
+            root = lax.rsqrt(square + FLOOR)
+            h = [g0 * root, g1 * root, g2 * root]
+            hh = square * root * root
             base = first[r, pl.ds(8 * j, 8)]
-            temporal = 2.0 * (avg[r + 1, pl.ds(s, 8)] - base)
-            source = [-n0 * temporal, -n1 * temporal, -n2 * temporal]
-            for k in range(6):
-                tensors[0][k, r, pl.ds(8 * j, 8)] = tensor[k]
-            for k in range(3):
-                sources[0][k, r, pl.ds(8 * j, 8)] = source[k]
+            time = (4.0 * root) * (avg[r + 1, pl.ds(s, 8)] - base)
+            for k, value in enumerate((*h, time, hh)):
+                moved[k, r, pl.ds(8 * j, 8)] = value
             total = below + above + (flags[0] + flags[1])
             total = total + (first_column if j == 0 else 1.0)
             total = total + (last_column if j == across // 8 - 1 else 1.0)
-            solved = solve_three(tensor, TIKHONOV + total, source)
-            store_chunk(0, 0, r, j, [RELAXATION * x for x in solved])
+            length = time * (-RELAXATION / (TIKHONOV + total + hh))
+            store_chunk(0, 0, r, j, [g * length for g in h])
+
+    def shrink_block(m):
+        shrink_motion([m * (ROWS // 2) + k for k in range(ROWS // 2)])
 
     def motion_block(m):
         for row in range(ROWS):
             motion(m * ROWS + row)
+        shrink_block(m)
 
     def gather_step(s, carry):
+        @pl.when(s + AHEAD < chunks)
+        def _():
+            send_own(s + AHEAD, 0)
+
         def chunk_at(t):
             return (t + chunks - 1) % chunks
 
@@ -682,8 +793,13 @@
         return carry
 
     lax.fori_loop(0, chunks + 2, gather_step, 0)
-    motion_block(chunks - 2)
+    for row in range(ROWS):
+        motion((chunks - 2) * ROWS + row)
     motion(height - ROWS)
+    arriving = exchange(0, 0)
+    start_all(arriving)
+    shrink_block(chunks - 2)
+    shrink_block(chunks - 1)
 
     def finish_sends(c, carry):
         for condition, copy in own_copies(c):
@@ -696,13 +812,11 @@
         return carry
 
     lax.fori_loop(0, chunks, finish_sends, 0)
-
-    current = exchange(0, 0)
-    start_all(current)
-    for l in range(LEVELS - 1):
-        shrink_array(l, 6, tensors[l], tensors[l + 1])
-    wait_all(current)
-    relax(0, 0, 1)
+    for l in range(1, LEVELS - 1):
+        shrink_array(l, tensors[l], tensors[l + 1], 0.125)
+    relax(0, 0, 1, "inner")
+    wait_all(arriving)
+    relax(0, 0, 1, "edge")
     for l in range(LEVELS - 1):
         b = 1 if l == 0 else 2
         current = exchange(l, b)
@@ -710,9 +824,11 @@
         shrink_iterate(l, b)
         following = exchange(l + 1, 0)
         start_all(following)
+        if l == 0:
+            residue(l, b, "inner")
         wait_all(current)
-        residue(l, b)
-        shrink_array(l, 3, residues[l], sources[l + 1])
+        residue(l, b, "edge" if l == 0 else "all")
+        shrink_array(l, residues[l], sources[l + 1], 0.0625 if l == 0 else 0.125)
         wait_all(following)
         enter(l + 1)
         current = exchange(l + 1, 1)
@@ -721,13 +837,23 @@
         relax(l + 1, 1, 2)
     for l in range(LEVELS - 2, -1, -1):
         b = 1 if l == 0 else 2
-        grow(l, b, 2 if l == LEVELS - 2 else 5, b + 1)
-        for sweep in range(2):
-            current = exchange(l, b + 1 + sweep)
+        solved = 2 if l == LEVELS - 2 else 5
+        arriving = exchange(l + 1, solved)
+        start_all(arriving)
+        grow(l, b, solved, b + 1, arriving)
+        if l > 0:
+            relax(l, b + 1, b + 2)
+            current = exchange(l, b + 2)
             start_all(current)
             wait_all(current)
-            last = l == 0 and sweep == 1
-            relax(l, b + 1 + sweep, None if last else b + 2 + sweep)
+            relax(l, b + 2, b + 3)
+    relax(0, 2, 3, "edge")
+    current = exchange(0, 3)
+    start_all(current)
+    relax(0, 2, 3, "inner")
+    relax(0, 3, None, "inner")
+    wait_all(current)
+    relax(0, 3, None, "edge")
 
 
 def body(n_gy, n_gx, first_frame, second_frame, source_column):
@@ -736,7 +862,7 @@
     hs = [height >> l for l in range(LEVELS)]
     wqs = [max(across >> l, 8) for l in range(LEVELS)]
     hqs = [max(h, 8) for h in hs]
-    total = sum(EXCHANGES) * 4
+    total = sum(BUFFERS) * 4
     vmem = pl.BlockSpec(memory_space=pltpu.VMEM)
     chunks = height // ROWS
     layered = n_gx == 2 * LAYERS
@@ -749,13 +875,13 @@
         pltpu.VMEM((chunks, 2, 8, LANES), f32),
         pltpu.VMEM((chunks, 2, 8, LANES), f32),
     ]
-    scratch += [pltpu.VMEM((6, hs[l], wqs[l], LANES), f32) for l in range(LEVELS)]
-    scratch += [pltpu.VMEM((3, hs[l], wqs[l], LANES), f32) for l in range(LEVELS)]
+    scratch += [pltpu.VMEM((6 if l else 5, hs[l], wqs[l], LANES), f32) for l in range(LEVELS)]
+    scratch += [pltpu.VMEM((3, hs[l], wqs[l], LANES), f32) for l in range(1, LEVELS)]
     scratch += [
         pltpu.VMEM((BUFFERS[l], 3, hs[l] + 2, wqs[l] + 2 * PAD, LANES), f32)
         for l in range(LEVELS)
     ]
-    scratch += [pltpu.VMEM((EXCHANGES[l], 2, 3, hqs[l], LANES), f32) for l in range(LEVELS)] * 2
+    scratch += [pltpu.VMEM((BUFFERS[l], 2, 3, hqs[l], LANES), f32) for l in range(LEVELS)] * 2
     scratch += [pltpu.VMEM((3, hs[l], wqs[l], LANES), f32) for l in range(LEVELS - 1)]
     dma = pltpu.SemaphoreType.DMA
     scratch += [dma((total,)), dma((total,)), dma((2,)), dma((2,)), dma]

time: 138 us -> 119 us (0.86)
  Pallas kernels: 135 us -> 116 us
    pallas_call x1, Pallas kernels: 135 us -> 116 us  [body(): pl.pallas_call(functools.partial(kernel, n_gy, n_gx, height, across), out...]
where the time goes in v2:
time: 119 us
  Pallas kernels  116 us (97%)
  local copies, waits for them, and re-layouts  2.67 us (2%)
    pallas_call x1, Pallas kernels, body(): pl.pallas_call(functools.partial(kernel, n_gy, n_gx, height, across), out...  116 us
    unnamed x1, local copies, waits for them, and re-layouts  2.67 us

profile of v2, /device:TPU:0, one launch (start us, length us, event | category | flops | bytes accessed | tf_op | source)
XLA Modules:
  0.0 118.7 jit_solution(11975320492332114124)
XLA Ops:
  0.0 116.0 %shard_map.37 = f32[3,32,32,128]{3,2,1,0:T(8,128)} custom-call(f32[32,32,128]{2,1,0:T(8,128)} %refs_0_.1, f32[32,32,128]{2,1,0:T(8,128)} %refs_1_.1, s32[4]{0:T(128)} %bitcast.1), custom_call_target="tpu_custom_call" | custom-call | tf_op jit(solution)/shard_map/pallas_call | solution.py:902
  116.0 2.7 %copy.5 = f32[3,32,32,128]{3,2,1,0:T(8,128)} copy(f32[3,32,32,128]{3,2,1,0:T(8,128)} %shard_map.37) | data formatting | bytes 3145728

commit v3 on v2

--- a/solution.py
+++ b/solution.py
@@ -19,6 +19,7 @@
 LAYERS = 4
 BUFFERS = (4, 6, 6, 3)
 AHEAD = 2
+CELLS = 16
 MESH = pl.DeviceIdType.MESH
 
 
@@ -415,7 +416,7 @@
 
     def sweep(l, b, start, count, js, group, compute, store):
         u = iterates[l]
-        first_column, last_column, _, above = masks[l]
+        first_column, last_column, below, above = masks[l]
         end = wqs[l] // 8 - 1
         scale = 0.25**l / (CONTRAST * CONTRAST) / (4.0 if l == 0 else 1.0)
 
@@ -448,7 +449,7 @@
                 else:
                     left = face(at(r, j, -1), center, first_column if j == 0 else None)
                 previous = right
-                back = [pltpu.roll(v, 1, 1) for v in side]
+                back = face([pltpu.roll(c, 1, 1) for c in center], center, below)
                 up = carry[n]
                 flux = [
                     (down[i] - up[i]) + (side[i] - back[i]) + (right[i] - left[i]) for i in range(3)
@@ -482,13 +483,13 @@
         h = hs[l]
         every = tuple(range(wqs[l] // 8))
         if which == "all":
-            sweep(l, b, 0, h, every, min(h, max(1, 4 // len(every))), compute, store)
+            sweep(l, b, 0, h, every, min(h, max(1, CELLS // len(every))), compute, store)
         elif which == "edge":
-            sweep(l, b, 0, h, (every[0], every[-1]), 2, compute, store)
+            sweep(l, b, 0, h, (every[0], every[-1]), CELLS // 2, compute, store)
             for r in (0, h - 1):
                 sweep(l, b, r, 1, every[1:-1], 1, compute, store)
         else:
-            sweep(l, b, 1, h - 2, every[1:-1], 2, compute, store)
+            sweep(l, b, 1, h - 2, every[1:-1], 6, compute, store)
 
     def motion_of(r, j):
         return [moved[k, r, pl.ds(8 * j, 8)] for k in range(5)]
@@ -906,7 +907,7 @@
         out_specs=vmem,
         scratch_shapes=scratch,
         compiler_params=pltpu.CompilerParams(
-            collective_id=0, has_side_effects=True, vmem_limit_bytes=56 * 1024 * 1024
+            collective_id=0, has_side_effects=True, vmem_limit_bytes=40 * 1024 * 1024
         ),
     )(first_frame, second_frame, columns)
 

time: 119 us -> 103 us (0.87)
  Pallas kernels: 116 us -> 99.3 us
  local copies, waits for them, and re-layouts: 2.67 us -> 3.88 us
    pallas_call x1, Pallas kernels: 116 us -> 99.3 us  [body(): pl.pallas_call(functools.partial(kernel, n_gy, n_gx, height, across), out...]
    unnamed x1 -> x7, local copies, waits for them, and re-layouts: 2.67 us -> 3.88 us
where the time goes in v3:
time: 103 us
  Pallas kernels  99.3 us (96%)
  local copies, waits for them, and re-layouts  3.88 us (4%)
    pallas_call x1, Pallas kernels, body(): pl.pallas_call(functools.partial(kernel, n_gy, n_gx, height, across), out...  99.3 us
    unnamed x7, local copies, waits for them, and re-layouts  3.88 us

profile of v3, /device:TPU:0, one launch (start us, length us, event | category | flops | bytes accessed | tf_op | source)
XLA Modules:
  0.0 103.2 jit_solution(2368985209556918108)
XLA Ops:
  0.0 0.0 copy-start
  0.0 1.0 %copy-done = f32[32,32,128]{2,1,0:T(8,128)S(1)} copy-done((f32[32,32,128]{2,1,0:T(8,128)S(1)}, f32[32,32,128]{2,1,0:T(8,128)}, u32[]{:S(2)}) %copy-start) | copy-done | bytes 524312
  1.0 0.0 copy-start.1
  1.0 1.0 %copy-done.1 = f32[32,32,128]{2,1,0:T(8,128)S(1)} copy-done((f32[32,32,128]{2,1,0:T(8,128)S(1)}, f32[32,32,128]{2,1,0:T(8,128)}, u32[]{:S(2)}) %copy-start.1) | copy-done | bytes 524312
  2.1 0.0 copy-start.2
  2.1 0.7 copy-done.2
  2.7 99.3 %shard_map.37 = f32[3,32,32,128]{3,2,1,0:T(8,128)S(1)} custom-call(f32[32,32,128]{2,1,0:T(8,128)S(1)} %copy-done, f32[32,32,128]{2,1,0:T(8,128)S(1)} %copy-done.1, s32[4]{0:T(128)S(1)} %bitcast.1), custom_call_target="tpu_custom_call" | custom-call | tf_op jit(solution)/shard_map/pallas_call | solution.py:903
  102.0 1.1 %copy.5 = f32[3,32,32,128]{3,2,1,0:T(8,128)} copy(f32[3,32,32,128]{3,2,1,0:T(8,128)S(1)} %shard_map.37) | data formatting | bytes 3145728
Async XLA Ops:
  0.0 1.0 %copy-start = (f32[32,32,128]{2,1,0:T(8,128)S(1)}, f32[32,32,128]{2,1,0:T(8,128)}, u32[]{:S(2)}) copy-start(f32[32,32,128]{2,1,0:T(8,128)} %refs_0_.1) | copy-start | bytes 1572868
  1.0 1.0 %copy-start.1 = (f32[32,32,128]{2,1,0:T(8,128)S(1)}, f32[32,32,128]{2,1,0:T(8,128)}, u32[]{:S(2)}) copy-start(f32[32,32,128]{2,1,0:T(8,128)} %refs_1_.1) | copy-start | bytes 1572868
  2.1 0.7 copy-start.2

commit v4 on v3

--- a/solution.py
+++ b/solution.py
@@ -60,7 +60,9 @@
 
 
 def kernel(n_gy, n_gx, height, across, *refs):
-    first, second, columns, out = refs[:4]
+    given, columns, out = refs[:3], refs[-1], refs[3]
+    first, second = refs[-3:-1]
+    refs = refs[:-3]
     cols, packets_in, packets_out, avg, avg_stage, avg_halo = refs[4:10]
     refs = refs[2:]
     moved = refs[8]
@@ -73,21 +75,19 @@
     residues = refs[28:31]
     halo_send, halo_recv, avg_send, avg_recv, own_sem = refs[31:36]
     mine, table, picks, table_send, table_recv = refs[36:41]
-    own_send, packet_send, col_recv, packet_recv, edge_send, edge_recv = refs[41:]
+    own_send, packet_send, col_recv, packet_recv, edge_send, edge_recv, load_sem = refs[41:]
     my_y, my_x = lax.axis_index("gy"), lax.axis_index("gx")
     bases = [sum(BUFFERS[:l]) * 4 for l in range(LEVELS)]
     hs = [height >> l for l in range(LEVELS)]
     ws = [across >> l for l in range(LEVELS)]
     wqs = [max(w, 8) for w in ws]
 
-    for l in range(LEVELS):
-        u, w, wq, h = iterates[l], ws[l], wqs[l], hs[l]
-        for b in range(BUFFERS[l]):
-            zero_row = jnp.zeros((3, wq + 2 * PAD, LANES), jnp.float32)
-            u[b, :, 0] = zero_row
-            u[b, :, h + 1] = zero_row
-            halos[l][b] = jnp.zeros(halos[l].shape[1:], jnp.float32)
-    iterates[LEVELS - 1][...] = jnp.zeros(iterates[LEVELS - 1].shape, jnp.float32)
+    loads = [
+        pltpu.make_async_copy(source, target, load_sem.at[k])
+        for k, (source, target) in enumerate(zip(given, (first, second, columns)))
+    ]
+    for load in loads:
+        load.start()
     avg[0] = jnp.zeros(avg.shape[1:], jnp.float32)
     avg[height + 1] = jnp.zeros(avg.shape[1:], jnp.float32)
     avg_halo[...] = jnp.zeros(avg_halo.shape, jnp.float32)
@@ -110,6 +110,8 @@
 
     peers = n_gx - 1 + jnp.where(has_up, 1, 0) + jnp.where(has_down, 1, 0)
     pl.semaphore_wait(barrier, peers)
+    for load in loads:
+        load.wait()
 
     def to_peer(step, source, target, send, recv):
         return pltpu.make_async_remote_copy(
@@ -248,6 +250,14 @@
         keep = pltpu.make_async_copy(second, cols.at[z], own_sem)
         pl.when(inner)(keep.start)
     lax.fori_loop(0, AHEAD, send_own, 0)
+    for l in range(LEVELS):
+        u, w, wq, h = iterates[l], ws[l], wqs[l], hs[l]
+        for b in range(BUFFERS[l]):
+            zero_row = jnp.zeros((3, wq + 2 * PAD, LANES), jnp.float32)
+            u[b, :, 0] = zero_row
+            u[b, :, h + 1] = zero_row
+            halos[l][b] = jnp.zeros(halos[l].shape[1:], jnp.float32)
+    iterates[LEVELS - 1][...] = jnp.zeros(iterates[LEVELS - 1].shape, jnp.float32)
 
     def wanted(entry):
         value = entry(0)
@@ -898,18 +908,22 @@
         dma((2, chunks)),
         dma((2, chunks)),
         dma((2, chunks)),
+        dma((3,)),
+        pltpu.VMEM(volume, f32),
+        pltpu.VMEM(volume, f32),
+        pltpu.SMEM((source_column.size,), jnp.int32),
     ]
     columns = source_column.reshape(-1)
     return pl.pallas_call(
         functools.partial(kernel, n_gy, n_gx, height, across),
         out_shape=jax.ShapeDtypeStruct((3, height, across, planes), f32),
-        in_specs=[vmem, vmem, pl.BlockSpec(memory_space=pltpu.SMEM)],
+        in_specs=[pl.BlockSpec(memory_space=pltpu.HBM)] * 3,
         out_specs=vmem,
         scratch_shapes=scratch,
         compiler_params=pltpu.CompilerParams(
             collective_id=0, has_side_effects=True, vmem_limit_bytes=40 * 1024 * 1024
         ),
-    )(first_frame, second_frame, columns)
+    )(*(pltpu.with_memory_space_constraint(x, pltpu.HBM) for x in (first_frame, second_frame, columns)))
 
 
 def solution(mesh):

time: 103 us -> 100 us (0.971)
  local copies, waits for them, and re-layouts: 3.88 us -> 1.15 us
    unnamed x7 -> x1, local copies, waits for them, and re-layouts: 3.88 us -> 1.15 us
where the time goes in v4:
time: 100 us; the launch traced here: 99.8 us
  Pallas kernels  98.7 us (99%)
  local copies, waits for them, and re-layouts  1.15 us (1%)
    pallas_call x1, Pallas kernels, body(): pl.pallas_call(functools.partial(kernel, n_gy, n_gx, height, across), out...  98.7 us

profile of v4, /device:TPU:0, one launch (start us, length us, event | category | flops | bytes accessed | tf_op | source)
XLA Modules:
  0.0 99.8 jit_solution(1105453018990069085)
XLA Ops:
  0.0 98.7 %shard_map.37 = f32[3,32,32,128]{3,2,1,0:T(8,128)S(1)} custom-call(f32[32,32,128]{2,1,0:T(8,128)} %refs_0_.1, f32[32,32,128]{2,1,0:T(8,128)} %refs_1_.1, s32[4]{0:T(128)} %bitcast.1), custom_call_target="tpu_custom_call" | custom-call | tf_op jit(solution)/shard_map/pallas_call | solution.py:917
  98.7 1.1 %copy.5 = f32[3,32,32,128]{3,2,1,0:T(8,128)} copy(f32[3,32,32,128]{3,2,1,0:T(8,128)S(1)} %shard_map.37) | data formatting | bytes 3145728

commit v5 on v4

--- a/solution.py
+++ b/solution.py
@@ -295,7 +295,7 @@
             values = [cols[k, r] for k in range(LAYERS)]
             for i in range(3):
                 packets_out[i, r] = by_layer(values, layers[i])
-        for copy in packet_copies(c):
+        for copy in packet_copies(c)[::-1]:
             copy.start()
 
     def edges(c):
@@ -495,11 +495,11 @@
         if which == "all":
             sweep(l, b, 0, h, every, min(h, max(1, CELLS // len(every))), compute, store)
         elif which == "edge":
-            sweep(l, b, 0, h, (every[0], every[-1]), CELLS // 2, compute, store)
+            sweep(l, b, 0, h, (every[0], every[-1]), CELLS, compute, store)
             for r in (0, h - 1):
                 sweep(l, b, r, 1, every[1:-1], 1, compute, store)
         else:
-            sweep(l, b, 1, h - 2, every[1:-1], 6, compute, store)
+            sweep(l, b, 1, h - 2, every[1:-1], 10, compute, store)
 
     def motion_of(r, j):
         return [moved[k, r, pl.ds(8 * j, 8)] for k in range(5)]

time: 100 us -> 98.8 us (0.988)
  Pallas kernels: 98.7 us -> 97.5 us
    pallas_call x1, Pallas kernels: 98.7 us -> 97.5 us  [body(): pl.pallas_call(functools.partial(kernel, n_gy, n_gx, height, across), out...]
where the time goes in v5:
time: 98.8 us; the launch traced here: 98.7 us
  Pallas kernels  97.5 us (99%)
  local copies, waits for them, and re-layouts  1.15 us (1%)
    pallas_call x1, Pallas kernels, body(): pl.pallas_call(functools.partial(kernel, n_gy, n_gx, height, across), out...  97.5 us

profile of v5, /device:TPU:0, one launch (start us, length us, event | category | flops | bytes accessed | tf_op | source)
XLA Modules:
  0.0 98.7 jit_solution(12061296184078031953)
XLA Ops:
  0.0 97.5 %shard_map.37 = f32[3,32,32,128]{3,2,1,0:T(8,128)S(1)} custom-call(f32[32,32,128]{2,1,0:T(8,128)} %refs_0_.1, f32[32,32,128]{2,1,0:T(8,128)} %refs_1_.1, s32[4]{0:T(128)} %bitcast.1), custom_call_target="tpu_custom_call" | custom-call | tf_op jit(solution)/shard_map/pallas_call | solution.py:917
  97.6 1.1 %copy.5 = f32[3,32,32,128]{3,2,1,0:T(8,128)} copy(f32[3,32,32,128]{3,2,1,0:T(8,128)S(1)} %shard_map.37) | data formatting | bytes 3145728
